TPU v7x, 256 devices: a whole 4x4x8 slice. The times are simulated.
256 devices in a mesh: scene: 2 (over core), ctx: 16 (over y, x), tp: 8 (over z).
Axes of the slice: x: 4, y: 4, z: 8, core: 2. Of those that a mesh axis runs over, the one named last changes fastest.
Arguments:
- queries: bfloat16 [4096, 8192], P(('scene', 'ctx'), 'tp'), parts along dimension 0, may hold values from -6 to 6
- prefix_keys: bfloat16 [32768, 1024], P(('scene', 'ctx'), 'tp'), parts along dimension 0, may hold values from -8 to 8
- scene_prefix_values: bfloat16 [32768, 1024], P(('scene', 'ctx'), 'tp'), parts along dimension 0, may hold values from -48 to 48
- question_token_keys: bfloat16 [4096, 1024], P(('scene', 'ctx'), 'tp'), parts along dimension 0, may hold values from -12 to 12
- question_token_values: bfloat16 [4096, 1024], P(('scene', 'ctx'), 'tp'), parts along dimension 0, may hold values from -48 to 48
- lengths: int32 [32], P(('scene', 'ctx')), parts along dimension 0, may hold values from 1 to 128, 1280 in all
Outputs:
- attention: bfloat16 [4096, 8192], P(('scene', 'ctx'), 'tp'), parts along dimension 0
There are 2 independent parts, one for each index of `scene`. A program takes and returns all parts, laid end to end along the dimension named above; each array names one. Nothing has to cross between parts.
Inputs may be any that keep to these rules, and one draw needn't show every extreme that they name: Each span holds at least one question token, and some span is full with 128; the sum is taken per scene: the 16 lengths of one scene add up to 1280, so the whole array over all scenes sums to that times the number of scenes.
All inputs are finite; a program needn't handle non-finite values. No bound on the sum of `lengths` on one device may be relied on, other than what follows from the above.
Results may differ from a plain program's by a relative error of at most 0.015.
Values may be sent and summed in bfloat16 or wider, within the bound.
A program may use at most 64 MiB of HBM per device.

v0:
```python
import math

import jax
import jax.numpy as jnp
from jax import lax
from jax.sharding import PartitionSpec as P

QUERY_HEADS = 64
KEY_VALUE_HEADS = 8
HEAD_WIDTH = 128


def absorb(partial_value, query_block, key_block, value_block):
    row_peak, row_total, weighted = partial_value
    scores = jnp.einsum(
        "kqd,pkd->kqp", query_block, key_block, preferred_element_type=jnp.float32
    ) * (1.0 / math.sqrt(HEAD_WIDTH))
    new_peak = jnp.maximum(row_peak, jnp.max(scores, axis=2))
    factor = jnp.exp(row_peak - new_peak)
    weights = jnp.exp(scores - new_peak[..., None])
    row_total = factor * row_total + jnp.sum(weights, axis=2)
    weighted = factor[..., None] * weighted + jnp.einsum(
        "kqp,pkd->kqd",
        weights.astype(jnp.bfloat16),
        value_block,
        preferred_element_type=jnp.float32,
    )
    return (new_peak, row_total, weighted)


def own_partial(stacked, question_token_keys, question_token_values, length):
    row_count = question_token_keys.shape[0]
    kv_local = stacked.shape[0]
    queries_per_group = stacked.shape[1] // row_count
    key_block = question_token_keys.reshape(row_count, kv_local, HEAD_WIDTH)
    value_block = question_token_values.reshape(row_count, kv_local, HEAD_WIDTH)
    scores = jnp.einsum("kqd,jkd->kqj", stacked, key_block, preferred_element_type=jnp.float32) * (
        1.0 / math.sqrt(HEAD_WIDTH)
    )
    token = jnp.arange(stacked.shape[1]) // queries_per_group
    column = jnp.arange(row_count)
    visible = (column[None, :] <= token[:, None]) & (column[None, :] < length)
    scores = jnp.where(visible[None], scores, -jnp.inf)
    row_peak = jnp.max(scores, axis=2)
    weights = jnp.exp(scores - row_peak[..., None])
    weighted = jnp.einsum(
        "kqj,jkd->kqd",
        weights.astype(jnp.bfloat16),
        value_block,
        preferred_element_type=jnp.float32,
    )
    return (row_peak, jnp.sum(weights, axis=2), weighted)


def shards(
    queries, prefix_keys, scene_prefix_values, question_token_keys, question_token_values, lengths
):
    row_count = queries.shape[0]
    kv_local = question_token_keys.shape[1] // HEAD_WIDTH
    queries_per_group = QUERY_HEADS // KEY_VALUE_HEADS
    shard_rows = prefix_keys.shape[0]
    stacked = (
        queries.reshape(row_count, kv_local, queries_per_group, HEAD_WIDTH)
        .transpose(1, 0, 2, 3)
        .reshape(kv_local, row_count * queries_per_group, HEAD_WIDTH)
    )
    length = lengths[0]
    own = own_partial(stacked, question_token_keys, question_token_values, length)
    partial_value = own
    key_piece = lax.all_gather(prefix_keys, "ctx", axis=0, tiled=True)
    value_piece = lax.all_gather(scene_prefix_values, "ctx", axis=0, tiled=True)
    piece_rows = key_piece.shape[0]
    key_piece = key_piece.reshape(piece_rows, kv_local, HEAD_WIDTH)
    value_piece = value_piece.reshape(piece_rows, kv_local, HEAD_WIDTH)
    key_parts = key_piece.reshape(piece_rows // shard_rows, shard_rows, kv_local, HEAD_WIDTH)
    value_parts = value_piece.reshape(piece_rows // shard_rows, shard_rows, kv_local, HEAD_WIDTH)

    def step_shard(inner, parts):
        return (absorb(inner, stacked, parts[0], parts[1]), None)

    partial_value, unused = lax.scan(step_shard, partial_value, (key_parts, value_parts))
    result = partial_value[2] / partial_value[1][..., None]
    result = (
        result.reshape(kv_local, row_count, queries_per_group, HEAD_WIDTH)
        .transpose(1, 0, 2, 3)
        .reshape(row_count, kv_local * queries_per_group * HEAD_WIDTH)
    )
    live_rows = jnp.arange(row_count) < length
    return jnp.where(live_rows[:, None], result, 0.0).astype(jnp.bfloat16)


def solution(mesh):
    return jax.shard_map(
        shards,
        mesh=mesh,
        in_specs=(
            P(("scene", "ctx"), "tp"),
            P(("scene", "ctx"), "tp"),
            P(("scene", "ctx"), "tp"),
            P(("scene", "ctx"), "tp"),
            P(("scene", "ctx"), "tp"),
            P(("scene", "ctx")),
        ),
        out_specs=P(("scene", "ctx"), "tp"),
        check_vma=False,
    )
```

profile of v0, /device:TPU:1, one launch (start us, length us, event | category | flops | bytes accessed | tf_op | source)
XLA Modules:
  0.0 207.5 jit_solution(9834465344585492850)
XLA Ops:
  12.2 57.9 %all-gather.3.cloned.1.call-done = bf16[16384,128]{1,0:T(8,128)(2,1)} async-done(((bf16[1024,128]{1,0:T(8,128)(2,1)}), bf16[16384,128]{1,0:T(8,128)(2,1)}) %all-gather.3.cloned.1.call-update) | async-done | bytes 4194320 | tf_op jit(solution)/shard_map/all_gather | solution.py:70
  70.2 58.7 %all-gather.5.cloned.1.call-done = bf16[16384,128]{1,0:T(8,128)(2,1)} async-done(((bf16[1024,128]{1,0:T(8,128)(2,1)}), bf16[16384,128]{1,0:T(8,128)(2,1)}) %all-gather.5.cloned.1.call-update) | async-done | bytes 4194320 | tf_op jit(solution)/shard_map/all_gather | solution.py:71
  128.9 70.5 %while.14 = (s32[]{:T(128)}, f32[1,1024]{1,0:T(1,128)S(1)}, f32[1,1024]{1,0:T(1,128)S(1)}, f32[1,1024,128]{2,1,0:T(8,128)S(1)}, bf16[16,1024,1,128]{3,1,2,0:T(8,...) while((s32[]{:T(128)}, f32[1,1024]{1,0:T(1,128)S(1)}, ...), condition=%wide.region_5.6_spmd, body=%wide.region_2.5_spmd.sunk | while | flops 545523712 | bytes 14484565 | solution.py:81
  131.4 1.9 fusion.41
  135.8 1.9 fusion.41
  137.7 1.7 multiply_reduce_fusion.2
  140.2 1.9 fusion.41
  144.6 1.9 fusion.41
  146.6 1.7 multiply_reduce_fusion.2
  149.0 1.9 fusion.41
  153.4 1.9 fusion.41
  157.8 1.9 fusion.41
  159.8 1.7 multiply_reduce_fusion.2
  162.2 1.9 fusion.41
  166.6 1.9 fusion.41
  171.0 1.9 fusion.41
  173.0 1.7 multiply_reduce_fusion.2
  175.5 1.9 fusion.41
  179.9 1.9 fusion.41
  184.3 1.9 fusion.41
  186.2 1.7 multiply_reduce_fusion.2
  188.7 1.9 fusion.41
  193.1 1.9 fusion.41
  197.5 1.9 fusion.41
  (91 shorter events, 36.6 us)
Async XLA Ops:
  6.5 4.3 %copy-start = (bf16[128,128]{1,0:T(8,128)(2,1)S(1)}, bf16[128,128]{1,0:T(8,128)(2,1)}, u32[]{:S(2)}) copy-start(bf16[128,128]{1,0:T(8,128)(2,1)} %param.11) | copy-start | bytes 98308
  6.5 63.6 %all-gather.3.cloned.1.call-start = ((), (), s32[]{:S(2)}) async-start(), calls=%async_computation | async-start | bytes 4456448 | tf_op jit(solution)/shard_map/all_gather | solution.py:70
  7.3 121.7 %all-gather.5.cloned.1.call-start = ((), (), s32[]{:S(2)}) async-start(), calls=%async_computation.1 | async-start | bytes 4456448 | tf_op jit(solution)/shard_map/all_gather | solution.py:71
Sparse Core Ops, SparseCore 0:
  9.8 60.3 all-gather.2
  72.6 56.2 all-gather.4
where the time goes:
time: 209 us; the launch traced here: 207 us
  waiting for transfers between devices  118 us (56%)
  matrix products  59 us (28%)
  between operations  14.1 us (7%)
  other arithmetic  13.3 us (6%)
  local copies, waits for them, and re-layouts  2.3 us (1%)
    all_gather x1, waiting for transfers between devices, shards(): value_piece = lax.all_gather(scene_prefix_values, 'ctx', axis=0, tiled=True)  58.7 us
    all_gather x1, waiting for transfers between devices, shards(): key_piece = lax.all_gather(prefix_keys, 'ctx', axis=0, tiled=True)  57.9 us
    dot_general x16, matrix products, absorb(): jnp.einsum('kqp,pkd->kqd', weights.astype(jnp.bfloat16), value_block, pre...  31 us
    dot_general x16, matrix products, absorb(): jnp.einsum('kqd,pkd->kqp', query_block, key_block, preferred_element_type...  26.6 us
    reduce_sum x16, other arithmetic, absorb(): row_total = factor * row_total + jnp.sum(weights, axis=2)  11.7 us
  transfers between devices with their start and end apart: 2, of which 2 were waited for; matrix products, arithmetic and copies ran while one was open for 2% of the time, Pallas kernels for 0%

commit v1 on v0

v1 whole, which is shorter than its diff:
```python
import functools
import math

import jax
import jax.numpy as jnp
from jax import lax
from jax.experimental import pallas as pl
from jax.experimental.pallas import tpu as pltpu
from jax.sharding import PartitionSpec as P

MESH = pl.DeviceIdType.MESH
F32, BF16 = jnp.float32, jnp.bfloat16
D = 128
H = 8
T = 128
ROWS = 1024
HALF = 512
SIDE = 4
EXTRA = 16
SCALE = math.log2(math.e) / math.sqrt(D)


def block_of(i):
    inner = lax.div(i + 15, 16)
    tail = lax.div(i, 13)
    pair = lax.div(i + 2, 3) - 1
    place = lax.rem(i + 2, 3)
    slot = 1 + place + lax.div(pair + 1, 4) * (2 - 2 * place)
    middle = inner * (1 - tail)
    return middle * slot, middle * pair + tail * (i - 12)


def kernel(q_in, k_in, v_in, ok_in, ov_in, len_ref, out_ref,
           q, kv, acc, mx, sm, s0, s1, x0, x1,
           o_send, st_send, f_recv, fst_recv, o_recv, ost_recv,
           q_ssem, q_rsem, kv_ssem, kv_rsem, o_ssem, o_rsem, st_ssem, st_rsem):
    me = lax.axis_index("ctx")
    y, x = lax.div(me, SIDE), lax.rem(me, SIDE)
    right = y * SIDE + lax.rem(x + 1, SIDE)
    left = y * SIDE + lax.rem(x + SIDE - 1, SIDE)
    up = lax.rem(y + 1, SIDE) * SIDE + x
    down = lax.rem(y + SIDE - 1, SIDE) * SIDE + x

    barrier = pltpu.get_barrier_semaphore()
    for other in (left, right, up, down):
        pl.semaphore_signal(barrier, inc=1, device_id={"ctx": other}, device_id_type=MESH)

    def remote(src, dst, ssem, rsem, to):
        return pltpu.make_async_remote_copy(
            src_ref=src, dst_ref=dst, send_sem=ssem, recv_sem=rsem,
            device_id={"ctx": to}, device_id_type=MESH)

    def q_copy(n):
        src, half, dst, to = ((0, 0, 1, right), (0, 1, 2, left), (0, 1, 1, right), (0, 0, 2, left),
                              (1, 0, 3, right), (2, 1, 3, left))[n]
        return remote(q.at[src, half], q.at[dst, half], q_ssem.at[n], q_rsem.at[n], to)

    def kv_copy(n):
        src, dst, to = ((0, 2, up), (1, 3, down), (1, 4, up), (0, 5, down), (2, 6, up), (3, 7, down))[n]
        return remote(kv.at[src], kv.at[dst], kv_ssem.at[n], kv_rsem.at[n], to)

    def o_copy(n):
        to = (right, left, right, right, left, left)[n]
        if n < 2:
            od, sd = f_recv.at[n], fst_recv.at[n]
        else:
            od, sd = o_recv.at[n - 2], ost_recv.at[n - 2]
        return (remote(o_send.at[n], od, o_ssem.at[n], o_rsem.at[n], to),
                remote(st_send.at[n], sd, st_ssem.at[n], st_rsem.at[n], to))

    def start_o(n):
        for c in o_copy(n):
            c.start()

    def wait_o(n):
        for c in o_copy(n):
            c.wait_recv()

    def transposed(a):
        return a.astype(F32).T.astype(BF16)

    for h in range(H):
        q[0, h // 4, :, (h % 4) * T:(h % 4 + 1) * T] = transposed(q_in[:, h * D:(h + 1) * D])
    pl.semaphore_wait(barrier, 4)
    for n in range(4):
        q_copy(n).start()
    for c in range(2):
        kv[c, 0:HALF, :] = k_in[c * HALF:(c + 1) * HALF, :]
        for b in range(HALF // 128):
            lo = c * HALF + b * 128
            kv[c, HALF + b * 128:HALF + (b + 1) * 128, :] = transposed(v_in[lo:lo + 128, :])
    for n in range(4):
        kv_copy(n).start()

    def values_of(ref_blocks):
        vt = jnp.concatenate(ref_blocks, axis=1)
        return jnp.concatenate([vt, jnp.ones((EXTRA, vt.shape[1]), BF16)], axis=0)

    length = len_ref[0]
    own_v = values_of([transposed(ov_in[...])])
    key_at = lax.broadcasted_iota(jnp.int32, (T, HALF), 0)
    token = lax.rem(lax.broadcasted_iota(jnp.int32, (T, HALF), 1), T)
    visible = (key_at <= token) & (key_at < length)
    for u in range(2):
        s = jnp.dot(ok_in[...], q[0, u], preferred_element_type=F32)
        s = jnp.where(visible, s, -1e30)
        m = jnp.max(s, axis=0, keepdims=True)
        p = jnp.exp2(s * SCALE - m * SCALE)
        d = jnp.dot(own_v, p.astype(BF16), preferred_element_type=F32)
        acc[0, u] = d[:D]
        mx[0, u, 0:1] = m
        sm[0, u, 0:1] = d[D:D + 1]
        for s in range(1, 4):
            acc[s, u] = jnp.zeros((D, HALF), F32)
            mx[s, u, 0:1] = jnp.full((1, HALF), -1e30, F32)
            sm[s, u, 0:1] = jnp.zeros((1, HALF), F32)

    def scores(slot, chunk, u, s_ref, x_ref):
        s = jnp.dot(kv[chunk, 0:HALF, :], q[slot, u], preferred_element_type=F32)
        s_ref[u] = s
        x_ref[u] = jnp.broadcast_to(jnp.max(s, axis=0, keepdims=True), (8, HALF))

    def absorb(slot, chunk, u, s_ref, x_ref):
        vt = values_of([kv[chunk, HALF + b * 128:HALF + (b + 1) * 128, :] for b in range(HALF // 128)])
        m, l = mx[slot, u, 0:1], sm[slot, u, 0:1]
        new = jnp.maximum(m, x_ref[u, 0:1])
        p = jnp.exp2(s_ref[u] * SCALE - new * SCALE)
        a = jnp.exp2((m - new) * SCALE)
        d = jnp.dot(vt, p.astype(BF16), preferred_element_type=F32)
        sm[slot, u, 0:1] = l * a + d[D:D + 1]
        acc[slot, u] = acc[slot, u] * a + d[:D]
        mx[slot, u, 0:1] = new

    def block(i, last=False):
        slot, pair = block_of(i)
        for u in range(2):
            scores(slot, 2 * pair + 1, u, s1, x1)
            absorb(slot, 2 * pair, u, s0, x0)
        if not last:
            slot2, pair2 = block_of(i + 1)
        for u in range(2):
            if not last:
                scores(slot2, 2 * pair2, u, s0, x0)
            absorb(slot, 2 * pair + 1, u, s1, x1)

    def pack(n, slot, u):
        o_send[n] = acc[slot, u].astype(BF16)
        st_send[n, 0:1] = mx[slot, u, 0:1]
        st_send[n, 1:2] = sm[slot, u, 0:1]

    def merge(slot, u, o_ref, st_ref):
        m, l = mx[slot, u, 0:1], sm[slot, u, 0:1]
        m2, l2 = st_ref[0:1], st_ref[1:2]
        new = jnp.maximum(m, m2)
        a, a2 = jnp.exp2((m - new) * SCALE), jnp.exp2((m2 - new) * SCALE)
        acc[slot, u] = acc[slot, u] * a + o_ref[...].astype(F32) * a2
        sm[slot, u, 0:1] = l * a + l2 * a2
        mx[slot, u, 0:1] = new

    for u in range(2):
        scores(0, 0, u, s0, x0)

    def body(i, carry):
        @pl.when(i == 0)
        def _():
            q_copy(0).wait_recv()
            q_copy(4).start()
            q_copy(1).wait_recv()
            q_copy(5).start()
            q_copy(2).wait_recv()

        @pl.when(i == 1)
        def _():
            q_copy(3).wait_recv()

        @pl.when(i == 2)
        def _():
            q_copy(4).wait_recv()
            q_copy(5).wait_recv()

        @pl.when(i == 3)
        def _():
            kv_copy(0).wait_recv()
            kv_copy(4).start()
            kv_copy(1).wait_recv()
            kv_copy(5).start()

        @pl.when(i == 6)
        def _():
            kv_copy(2).wait_recv()
            kv_copy(3).wait_recv()

        @pl.when(i == 9)
        def _():
            kv_copy(4).wait_recv()
            kv_copy(5).wait_recv()

        @pl.when(i == 11)
        def _():
            for u in range(2):
                pack(u, 3, u)
                start_o(u)

        @pl.when(i == 12)
        def _():
            pack(2, 2, 1)
            start_o(2)

        @pl.when(i == 13)
        def _():
            pack(4, 1, 0)
            start_o(4)

        @pl.when(i == 14)
        def _():
            wait_o(0)
            merge(2, 0, f_recv.at[0], fst_recv.at[0])
            pack(3, 2, 0)
            start_o(3)
            wait_o(1)
            merge(1, 1, f_recv.at[1], fst_recv.at[1])
            pack(5, 1, 1)
            start_o(5)

        block(i)
        return carry

    lax.fori_loop(0, 15, body, 0)
    block(15, last=True)

    rows = lax.broadcasted_iota(jnp.int32, (T, D), 0)
    for u, a, b in ((0, 3, 4), (1, 2, 5)):
        for n in (a, b):
            wait_o(n)
            merge(0, u, o_recv.at[n - 2], ost_recv.at[n - 2])
        result = acc[0, u] / sm[0, u, 0:1]
        for h in range(4):
            piece = result[:, h * T:(h + 1) * T].T
            at = (u * 4 + h) * D
            out_ref[:, at:at + D] = jnp.where(rows < length, piece, 0.0).astype(BF16)

    for n in range(6):
        q_copy(n).wait_send()
        kv_copy(n).wait_send()
        for c in o_copy(n):
            c.wait_send()


def shards(queries, prefix_keys, prefix_values, own_keys, own_values, lengths):
    vmem = pl.BlockSpec(memory_space=pltpu.VMEM)
    dma = pltpu.SemaphoreType.DMA
    return pl.pallas_call(
        kernel,
        out_shape=jax.ShapeDtypeStruct((T, H * D), BF16),
        in_specs=[vmem] * 5 + [pl.BlockSpec(memory_space=pltpu.SMEM)],
        out_specs=vmem,
        scratch_shapes=[
            pltpu.VMEM((4, 2, D, HALF), BF16),
            pltpu.VMEM((8, 2 * HALF, D), BF16),
            pltpu.VMEM((4, 2, D, HALF), F32),
            pltpu.VMEM((4, 2, 8, HALF), F32),
            pltpu.VMEM((4, 2, 8, HALF), F32),
            pltpu.VMEM((2, HALF, HALF), F32),
            pltpu.VMEM((2, HALF, HALF), F32),
            pltpu.VMEM((2, 8, HALF), F32),
            pltpu.VMEM((2, 8, HALF), F32),
            pltpu.VMEM((6, D, HALF), BF16),
            pltpu.VMEM((6, 8, HALF), F32),
            pltpu.VMEM((2, D, HALF), BF16),
            pltpu.VMEM((2, 8, HALF), F32),
            pltpu.VMEM((4, D, HALF), BF16),
            pltpu.VMEM((4, 8, HALF), F32),
        ] + [dma((6,))] * 8,
        compiler_params=pltpu.CompilerParams(
            collective_id=0, has_side_effects=True, vmem_limit_bytes=40 * 2**20),
        cost_estimate=pl.CostEstimate(flops=8 * 4096 * 4096 * 64, bytes_accessed=2**21, transcendentals=2**24),
    )(queries, prefix_keys, prefix_values, own_keys, own_values, lengths)


def solution(mesh):
    rows = P(("scene", "ctx"), "tp")
    return jax.shard_map(
        shards,
        mesh=mesh,
        in_specs=(rows, rows, rows, rows, rows, P(("scene", "ctx"))),
        out_specs=rows,
        check_vma=False,
    )
```

time: 209 us -> 42.8 us (0.20)
  the two profiles are of different devices: /device:TPU:1 before, /device:TPU:32 now
where the time goes in v1:
time: 42.8 us; the launch traced here: 42.5 us
  Pallas kernels  36.8 us (86%)
  local copies, waits for them, and re-layouts  5.06 us (12%)
  between operations  0.67 us (2%)
    pallas_call x1, Pallas kernels, shards(): pl.pallas_call(kernel, out_shape=jax.ShapeDtypeStruct((T, H * D), BF16),...  36.8 us
    unnamed x11, local copies, waits for them, and re-layouts  5.06 us

profile of v1, /device:TPU:32, one launch (start us, length us, event | category | flops | bytes accessed | tf_op | source)
XLA Modules:
  0.0 42.5 jit_solution(10607144100019226714)
XLA Ops:
  0.7 0.0 copy-start
  0.7 0.9 %copy-done = bf16[128,1024]{1,0:T(8,128)(2,1)S(1)} copy-done((bf16[128,1024]{1,0:T(8,128)(2,1)S(1)}, bf16[128,1024]{1,0:T(8,128)(2,1)}, u32[]{:S(2)}) %copy-start) | copy-done | bytes 262168
  1.6 0.0 copy-start.1
  1.6 0.9 %copy-done.1 = bf16[1024,128]{1,0:T(8,128)(2,1)S(1)} copy-done((bf16[1024,128]{1,0:T(8,128)(2,1)S(1)}, bf16[1024,128]{1,0:T(8,128)(2,1)}, u32[]{:S(2)}) %copy-start.1) | copy-done | bytes 262168
  2.6 0.0 copy-start.2
  2.6 0.9 %copy-done.2 = bf16[1024,128]{1,0:T(8,128)(2,1)S(1)} copy-done((bf16[1024,128]{1,0:T(8,128)(2,1)S(1)}, bf16[1024,128]{1,0:T(8,128)(2,1)}, u32[]{:S(2)}) %copy-start.2) | copy-done | bytes 262168
  3.5 0.0 copy-start.3
  3.5 0.8 %copy-done.3 = bf16[128,128]{1,0:T(8,128)(2,1)S(1)} copy-done((bf16[128,128]{1,0:T(8,128)(2,1)S(1)}, bf16[128,128]{1,0:T(8,128)(2,1)}, u32[]{:S(2)}) %copy-start.3) | copy-done | bytes 32792
  4.3 0.0 copy-start.4
  4.3 0.8 %copy-done.4 = bf16[128,128]{1,0:T(8,128)(2,1)S(1)} copy-done((bf16[128,128]{1,0:T(8,128)(2,1)S(1)}, bf16[128,128]{1,0:T(8,128)(2,1)}, u32[]{:S(2)}) %copy-start.4) | copy-done | bytes 32792
  5.0 36.8 %shard_map.64 = bf16[128,1024]{1,0:T(8,128)(2,1)S(1)} custom-call(bf16[128,1024]{1,0:T(8,128)(2,1)S(1)} %copy-done, bf16[1024,128]{1,0:T(8,128)(2,1)S(1)} %copy-done.1, bf16[1024,128]{1,0:T(8,128)(2,1)S(1)} %copy-done.2, bf16[128,128]{1,0:T(8,128)(2,1)S(1)} %copy-done.3, bf16[128,128]{1,0:T(8,128)(2,1)S(1)} %copy-done.4, s32[1]{0:T(128)S(6)} %copy.8.len_ref), custom_call_target="tpu_custom_call" | custom-call | flops 8589934592 | bytes 2097152 | tf_op jit(solution)/shard_map/pallas_call | solution.py:252
  41.8 0.7 %copy.9 = bf16[128,1024]{1,0:T(8,128)(2,1)} copy(bf16[128,1024]{1,0:T(8,128)(2,1)S(1)} %shard_map.64) | data formatting | bytes 524288
Async XLA Ops:
  0.7 1.0 %copy-start = (bf16[128,1024]{1,0:T(8,128)(2,1)S(1)}, bf16[128,1024]{1,0:T(8,128)(2,1)}, u32[]{:S(2)}) copy-start(bf16[128,1024]{1,0:T(8,128)(2,1)} %q_in.1) | copy-start | bytes 786436
  1.6 0.9 %copy-start.1 = (bf16[1024,128]{1,0:T(8,128)(2,1)S(1)}, bf16[1024,128]{1,0:T(8,128)(2,1)}, u32[]{:S(2)}) copy-start(bf16[1024,128]{1,0:T(8,128)(2,1)} %k_in.1) | copy-start | bytes 786436
  2.6 0.9 %copy-start.2 = (bf16[1024,128]{1,0:T(8,128)(2,1)S(1)}, bf16[1024,128]{1,0:T(8,128)(2,1)}, u32[]{:S(2)}) copy-start(bf16[1024,128]{1,0:T(8,128)(2,1)} %v_in.1) | copy-start | bytes 786436
  3.5 0.8 %copy-start.3 = (bf16[128,128]{1,0:T(8,128)(2,1)S(1)}, bf16[128,128]{1,0:T(8,128)(2,1)}, u32[]{:S(2)}) copy-start(bf16[128,128]{1,0:T(8,128)(2,1)} %ok_in.1) | copy-start | bytes 98308
  4.3 0.8 %copy-start.4 = (bf16[128,128]{1,0:T(8,128)(2,1)S(1)}, bf16[128,128]{1,0:T(8,128)(2,1)}, u32[]{:S(2)}) copy-start(bf16[128,128]{1,0:T(8,128)(2,1)} %ov_in.1) | copy-start | bytes 98308

commit v2 on v0

v2 whole, which is shorter than its diff:
```python
import math

import jax
import jax.numpy as jnp
from jax import lax
from jax.experimental import pallas as pl
from jax.experimental.pallas import tpu as pltpu
from jax.sharding import PartitionSpec as P

MESH = pl.DeviceIdType.MESH
F32, BF16 = jnp.float32, jnp.bfloat16
D = 128
H = 8
T = 128
ROWS = 1024
HALF = 512
PART = 256
SIDE = 4
SCALE = math.log2(math.e) / math.sqrt(D)


ORDER = ((0, 0), (1, 0), (2, 0), (1, 1), (2, 1), (3, 0), (3, 1), (3, 2),
         (1, 2), (3, 3), (1, 3), (2, 2), (2, 3), (0, 1), (0, 2), (0, 3))
BLOCKS = len(ORDER)


def block_of(i):
    if isinstance(i, int):
        return ORDER[i]
    found = list(ORDER[0])
    for k in range(1, BLOCKS):
        reached = lax.div(i + (BLOCKS - k), BLOCKS)
        for part in range(2):
            step = ORDER[k][part] - ORDER[k - 1][part]
            if step:
                found[part] = found[part] + step * reached
    return found


def kernel(q_hbm, k_hbm, v_hbm, ok_hbm, ov_hbm, len_ref, out_ref,
           q, kb, vb, ok, ov, acc, mx, sm, s0, s1, x0, x1,
           o_send, st_send, o_recv, st_recv,
           in_sem, q_ssem, q_rsem, k_ssem, k_rsem, v_ssem, v_rsem, o_ssem, o_rsem, st_ssem, st_rsem):
    me = lax.axis_index("ctx")
    y, x = lax.div(me, SIDE), lax.rem(me, SIDE)
    turn = lax.axis_index("scene")

    def at(dx, dy):
        return lax.rem(y + dy, SIDE) * SIDE + lax.rem(x + dx, SIDE)

    right, left = at(1 - turn, turn), at((1 - turn) * 3, turn * 3)
    up, down = at(turn, 1 - turn), at(turn * 3, (1 - turn) * 3)
    far = at((1 - turn) * 2, turn * 2)

    def half(n):
        return pl.ds(n * HALF, HALF)

    loads = [
        pltpu.make_async_copy(q_hbm.at[:, half(0)], q.at[0], in_sem.at[0]),
        pltpu.make_async_copy(q_hbm.at[:, half(1)], q.at[1], in_sem.at[1]),
        pltpu.make_async_copy(k_hbm, kb.at[0], in_sem.at[2]),
        pltpu.make_async_copy(ok_hbm, ok, in_sem.at[3]),
        pltpu.make_async_copy(ov_hbm, ov, in_sem.at[4]),
        pltpu.make_async_copy(v_hbm, vb.at[0], in_sem.at[5]),
    ]
    for load in loads:
        load.start()
    barrier = pltpu.get_barrier_semaphore()
    for other in (left, right, up, down, far):
        pl.semaphore_signal(barrier, inc=1, device_id={"ctx": other}, device_id_type=MESH)

    def remote(src, dst, ssem, rsem, to):
        return pltpu.make_async_remote_copy(
            src_ref=src, dst_ref=dst, send_sem=ssem, recv_sem=rsem,
            device_id={"ctx": to}, device_id_type=MESH)

    def q_copy(n):
        dst, to = 2 + n, (right, left)[n % 2]
        src = q.at[n - 2] if n > 3 else q_hbm.at[:, half((0, 1, 1, 0)[n])]
        return remote(src, q.at[dst], q_ssem.at[n], q_rsem.at[n], to)

    def ring_copy(n, hbm, buf, ssem, rsem):
        place, to = half(n % 2), (up, down)[n % 2]
        src = buf.at[1, place] if n > 3 else hbm.at[half((0, 1, 1, 0)[n])]
        return remote(src, buf.at[1 + n // 2, place], ssem.at[n], rsem.at[n], to)

    def k_copy(n):
        return ring_copy(n, k_hbm, kb, k_ssem, k_rsem)

    def v_copy(n):
        return ring_copy(n, v_hbm, vb, v_ssem, v_rsem)

    def o_copy(n):
        to = (far, far, right, right, left, left)[n]
        return (remote(o_send.at[n], o_recv.at[n], o_ssem.at[n], o_rsem.at[n], to),
                remote(st_send.at[n], st_recv.at[n], st_ssem.at[n], st_rsem.at[n], to))

    def send_o(n, unit):
        o_send[n] = acc[unit].astype(BF16)
        for h in range(4):
            cols = slice(h * T, (h + 1) * T)
            st_send[n, h:h + 1, :] = mx[unit, 0:1, cols]
            st_send[n, 4 + h:5 + h, :] = sm[unit, 0:1, cols]
        for c in o_copy(n):
            c.start()

    def merge(unit, n):
        for c in o_copy(n):
            c.wait_recv()
        m, l = mx[unit, 0:1], sm[unit, 0:1]
        m2 = jnp.concatenate([st_recv[n, h:h + 1, :] for h in range(4)], axis=1)
        l2 = jnp.concatenate([st_recv[n, h:h + 1, :] for h in range(4, 8)], axis=1)
        new = jnp.maximum(m, m2)
        a, a2 = jnp.exp2((m - new) * SCALE), jnp.exp2((m2 - new) * SCALE)
        acc[unit] = acc[unit] * a + o_recv[n].astype(F32) * a2
        sm[unit, 0:1] = l * a + l2 * a2
        mx[unit, 0:1] = new

    def rows_of(unit, lo, hi):
        return jnp.concatenate([q[unit, :, h * D:(h + 1) * D] for h in range(lo, hi)], axis=0)

    def dot(a, b, da, db):
        return lax.dot_general(a, b, (((da,), (db,)), ((), ())), preferred_element_type=F32)

    def scores(i, u, s_ref, x_ref):
        slot, pair = block_of(i)
        cols = slice(u * PART, (u + 1) * PART)
        s = dot(kb[pair], rows_of(2 * slot + u // 2, 2 * (u % 2), 2 * (u % 2) + 2), 1, 1)
        s_ref[:, cols] = s
        x_ref[:, cols] = jnp.broadcast_to(jnp.max(s, axis=0, keepdims=True), (8, PART))

    def absorb(i, u, s_ref, x_ref):
        slot, pair = block_of(i)
        unit, cols = 2 * slot + u // 2, slice(u % 2 * PART, (u % 2 + 1) * PART)
        here = slice(u * PART, (u + 1) * PART)
        m, l = mx[unit, 0:1, cols], sm[unit, 0:1, cols]
        new = jnp.maximum(m, x_ref[0:1, here])
        p = jnp.exp2(s_ref[:, here] * SCALE - new * SCALE)
        a = jnp.exp2((m - new) * SCALE)
        d = dot(vb[pair], p.astype(BF16), 0, 0)
        sm[unit, 0:1, cols] = l * a + jnp.sum(p, axis=0, keepdims=True)
        acc[unit, :, cols] = acc[unit, :, cols] * a + d
        mx[unit, 0:1, cols] = new

    def block(i, cur, nxt):
        for u in range(4):
            if nxt is not None:
                scores(i + 1, u, *nxt)
            absorb(i, u, *cur)

    pl.semaphore_wait(barrier, 5)
    for n in range(4):
        q_copy(n).start()
    for n in range(2, 8):
        acc[n] = jnp.zeros((D, HALF), F32)
        mx[n, 0:1] = jnp.full((1, HALF), -1e30, F32)
        sm[n, 0:1] = jnp.zeros((1, HALF), F32)
    for n in range(5):
        loads[n].wait()

    length = len_ref[0]
    key_at = lax.broadcasted_iota(jnp.int32, (T, HALF), 0)
    token = lax.rem(lax.broadcasted_iota(jnp.int32, (T, HALF), 1), T)
    visible = (key_at <= token) & (key_at < length)
    for n in range(2):
        s = jnp.where(visible, dot(ok[...], rows_of(n, 0, 4), 1, 1), -1e30)
        m = jnp.max(s, axis=0, keepdims=True)
        p = jnp.exp2(s * SCALE - m * SCALE)
        acc[n] = dot(ov[...], p.astype(BF16), 0, 0)
        mx[n, 0:1] = m
        sm[n, 0:1] = jnp.sum(p, axis=0, keepdims=True)
    for u in range(4):
        scores(0, u, s0, x0)
    for n in range(4):
        k_copy(n).start()
        v_copy(n).start()
    loads[5].wait()

    even, odd = (s0, x0), (s1, x1)

    def receive(copy, *numbers):
        for n in numbers:
            copy(n).wait_recv()

    def q_needed(slot):
        if slot == 1:
            receive(q_copy, 0, 1)
            q_copy(4).start()
            q_copy(5).start()
        else:
            receive(q_copy, *((2, 3) if slot == 2 else (4, 5)))

    def ring_needed(copy, pair):
        receive(copy, 2 * pair - 2, 2 * pair - 1)
        if pair == 1:
            copy(4).start()
            copy(5).start()

    def send_slot(slot):
        for n, unit in (((2, 3), (4, 2)), ((3, 5), (5, 4)), ((0, 6), (1, 7)))[slot - 1]:
            send_o(n, unit)

    def before(i):
        todo = []
        if i > 0:
            done = ORDER[i - 1][0]
            if done > 0 and all(slot != done for slot, _ in ORDER[i:]):
                todo.append((send_slot, done))
        slot, pair = ORDER[i]
        if pair > 0 and all(p != pair for _, p in ORDER[:i]):
            todo.append((lambda p: ring_needed(v_copy, p), pair))
        if i + 1 < BLOCKS:
            slot, pair = ORDER[i + 1]
            if slot > 0 and all(t != slot for t, _ in ORDER[:i + 1]):
                todo.append((q_needed, slot))
            if pair > 0 and all(p != pair for _, p in ORDER[:i + 1]):
                todo.append((lambda p: ring_needed(k_copy, p), pair))
        return todo

    def body(j, carry):
        for parity, (cur, nxt) in enumerate(((even, odd), (odd, even))):
            for k in range(BLOCKS // 2 - 1):
                todo = before(2 * k + parity)
                if todo:
                    @pl.when(j == k)
                    def _():
                        for act, what in todo:
                            act(what)
            block(2 * j + parity, cur, nxt)
        return carry

    lax.fori_loop(0, BLOCKS // 2 - 1, body, 0)
    for i, cur, nxt in ((BLOCKS - 2, even, odd), (BLOCKS - 1, odd, None)):
        for act, what in before(i):
            act(what)
        block(i, cur, nxt)
    for unit, n in ((0, 0), (1, 1), (0, 4), (1, 2)):
        merge(unit, n)

    rows = lax.broadcasted_iota(jnp.int32, (T, D), 0)
    for unit, n in ((0, 3), (1, 5)):
        merge(unit, n)
        result = acc[unit] / sm[unit, 0:1]
        for h in range(4):
            piece = result[:, h * T:(h + 1) * T].T
            lo = (unit * 4 + h) * D
            out_ref[:, lo:lo + D] = jnp.where(rows < length, piece, 0.0).astype(BF16)

    for n in range(6):
        for c in (q_copy(n), k_copy(n), v_copy(n), *o_copy(n)):
            c.wait_send()


def shards(queries, prefix_keys, prefix_values, own_keys, own_values, lengths):
    dma = pltpu.SemaphoreType.DMA
    return pl.pallas_call(
        kernel,
        out_shape=jax.ShapeDtypeStruct((T, H * D), BF16),
        in_specs=[pl.BlockSpec(memory_space=pltpu.HBM)] * 5 + [pl.BlockSpec(memory_space=pltpu.SMEM)],
        out_specs=pl.BlockSpec(memory_space=pltpu.VMEM),
        scratch_shapes=[
            pltpu.VMEM((8, T, HALF), BF16),
            pltpu.VMEM((4, ROWS, D), BF16),
            pltpu.VMEM((4, ROWS, D), BF16),
            pltpu.VMEM((T, D), BF16),
            pltpu.VMEM((T, D), BF16),
            pltpu.VMEM((8, D, HALF), F32),
            pltpu.VMEM((8, 8, HALF), F32),
            pltpu.VMEM((8, 8, HALF), F32),
            pltpu.VMEM((ROWS, 2 * HALF), F32),
            pltpu.VMEM((ROWS, 2 * HALF), F32),
            pltpu.VMEM((8, 2 * HALF), F32),
            pltpu.VMEM((8, 2 * HALF), F32),
            pltpu.VMEM((6, D, HALF), BF16),
            pltpu.VMEM((6, 8, T), F32),
            pltpu.VMEM((6, D, HALF), BF16),
            pltpu.VMEM((6, 8, T), F32),
        ] + [dma((6,))] * 11,
        compiler_params=pltpu.CompilerParams(
            collective_id=0, has_side_effects=True, vmem_limit_bytes=62 * 2**20),
        cost_estimate=pl.CostEstimate(flops=2**33, bytes_accessed=2**21, transcendentals=2**24),
    )(queries, prefix_keys, prefix_values, own_keys, own_values, lengths)


def solution(mesh):
    rows = P(("scene", "ctx"), "tp")
    return jax.shard_map(
        shards,
        mesh=mesh,
        in_specs=(rows, rows, rows, rows, rows, P(("scene", "ctx"))),
        out_specs=rows,
        check_vma=False,
    )
```

time: 209 us -> 36 us (0.17)
  the two profiles are of different devices: /device:TPU:1 before, /device:TPU:192 now
where the time goes in v2:
time: 36 us; the launch traced here: 35.9 us
  Pallas kernels  33.5 us (93%)
  local copies, waits for them, and re-layouts  1.67 us (5%)
  between operations  0.66 us (2%)
    pallas_call x1, Pallas kernels, shards(): pl.pallas_call(kernel, out_shape=jax.ShapeDtypeStruct((T, H * D), BF16),...  33.5 us
    unnamed x1, local copies, waits for them, and re-layouts  1.67 us

profile of v2, /device:TPU:192, one launch (start us, length us, event | category | flops | bytes accessed | tf_op | source)
XLA Modules:
  0.0 35.9 jit_solution(12445838035395134082)
XLA Ops:
  0.7 33.5 %shard_map.64 = bf16[128,1024]{1,0:T(8,128)(2,1)} custom-call(bf16[128,1024]{1,0:T(8,128)(2,1)} %q_hbm.1, bf16[1024,128]{1,0:T(8,128)(2,1)} %k_hbm.1, bf16[1024,128]{1,0:T(8,128)(2,1)} %v_hbm.1, bf16[128,128]{1,0:T(8,128)(2,1)} %ok_hbm.1, bf16[128,128]{1,0:T(8,128)(2,1)} %ov_hbm.1, s32[1]{0:T(128)S(6)} %copy.8.len_ref), custom_call_target="tpu_custom_call" | custom-call | flops 8589934592 | bytes 2097152 | tf_op jit(solution)/shard_map/pallas_call | solution.py:256
  34.2 1.7 %copy.9 = bf16[128,1024]{1,0:T(8,128)(2,1)} copy(bf16[128,1024]{1,0:T(8,128)(2,1)} %shard_map.64) | data formatting | bytes 524288

commit v3 on v2

--- a/solution.py
+++ b/solution.py
@@ -37,8 +37,8 @@
     return found
 
 
-def kernel(q_hbm, k_hbm, v_hbm, ok_hbm, ov_hbm, len_ref, out_ref,
-           q, kb, vb, ok, ov, acc, mx, sm, s0, s1, x0, x1,
+def kernel(q_hbm, k_hbm, v_hbm, okv_hbm, len_hbm, out_hbm,
+           len_ref, out, q, kb, vb, ok, ov, acc, mx, sm, s0, s1, x0, x1,
            o_send, st_send, o_recv, st_recv,
            in_sem, q_ssem, q_rsem, k_ssem, k_rsem, v_ssem, v_rsem, o_ssem, o_rsem, st_ssem, st_rsem):
     me = lax.axis_index("ctx")
@@ -59,9 +59,10 @@
         pltpu.make_async_copy(q_hbm.at[:, half(0)], q.at[0], in_sem.at[0]),
         pltpu.make_async_copy(q_hbm.at[:, half(1)], q.at[1], in_sem.at[1]),
         pltpu.make_async_copy(k_hbm, kb.at[0], in_sem.at[2]),
-        pltpu.make_async_copy(ok_hbm, ok, in_sem.at[3]),
-        pltpu.make_async_copy(ov_hbm, ov, in_sem.at[4]),
-        pltpu.make_async_copy(v_hbm, vb.at[0], in_sem.at[5]),
+        pltpu.make_async_copy(okv_hbm.at[pl.ds(0, T)], ok, in_sem.at[3]),
+        pltpu.make_async_copy(okv_hbm.at[pl.ds(T, T)], ov, in_sem.at[4]),
+        pltpu.make_async_copy(len_hbm, len_ref, in_sem.at[5]),
+        pltpu.make_async_copy(v_hbm, vb.at[0], in_sem.at[6]),
     ]
     for load in loads:
         load.start()
@@ -155,7 +156,7 @@
         acc[n] = jnp.zeros((D, HALF), F32)
         mx[n, 0:1] = jnp.full((1, HALF), -1e30, F32)
         sm[n, 0:1] = jnp.zeros((1, HALF), F32)
-    for n in range(5):
+    for n in range(6):
         loads[n].wait()
 
     length = len_ref[0]
@@ -174,7 +175,7 @@
     for n in range(4):
         k_copy(n).start()
         v_copy(n).start()
-    loads[5].wait()
+    loads[6].wait()
 
     even, odd = (s0, x0), (s1, x1)
 
@@ -238,13 +239,18 @@
         merge(unit, n)
 
     rows = lax.broadcasted_iota(jnp.int32, (T, D), 0)
+    writes = []
     for unit, n in ((0, 3), (1, 5)):
         merge(unit, n)
         result = acc[unit] / sm[unit, 0:1]
         for h in range(4):
             piece = result[:, h * T:(h + 1) * T].T
-            lo = (unit * 4 + h) * D
-            out_ref[:, lo:lo + D] = jnp.where(rows < length, piece, 0.0).astype(BF16)
+            out[:, (unit * 4 + h) * D:(unit * 4 + h + 1) * D] = jnp.where(rows < length, piece, 0.0).astype(BF16)
+        write = pltpu.make_async_copy(out.at[:, half(unit)], out_hbm.at[:, half(unit)], in_sem.at[7 + unit])
+        write.start()
+        writes.append(write)
+    for write in writes:
+        write.wait()
 
     for n in range(6):
         for c in (q_copy(n), k_copy(n), v_copy(n), *o_copy(n)):
@@ -256,9 +262,11 @@
     return pl.pallas_call(
         kernel,
         out_shape=jax.ShapeDtypeStruct((T, H * D), BF16),
-        in_specs=[pl.BlockSpec(memory_space=pltpu.HBM)] * 5 + [pl.BlockSpec(memory_space=pltpu.SMEM)],
-        out_specs=pl.BlockSpec(memory_space=pltpu.VMEM),
+        in_specs=[pl.BlockSpec(memory_space=pltpu.HBM)] * 5,
+        out_specs=pl.BlockSpec(memory_space=pltpu.HBM),
         scratch_shapes=[
+            pltpu.SMEM((1,), jnp.int32),
+            pltpu.VMEM((T, H * D), BF16),
             pltpu.VMEM((8, T, HALF), BF16),
             pltpu.VMEM((4, ROWS, D), BF16),
             pltpu.VMEM((4, ROWS, D), BF16),
@@ -275,11 +283,11 @@
             pltpu.VMEM((6, 8, T), F32),
             pltpu.VMEM((6, D, HALF), BF16),
             pltpu.VMEM((6, 8, T), F32),
-        ] + [dma((6,))] * 11,
+        ] + [dma((9,))] + [dma((6,))] * 10,
         compiler_params=pltpu.CompilerParams(
-            collective_id=0, has_side_effects=True, vmem_limit_bytes=62 * 2**20),
+            collective_id=0, has_side_effects=True, vmem_limit_bytes=5355 * 2**20 // 100),
         cost_estimate=pl.CostEstimate(flops=2**33, bytes_accessed=2**21, transcendentals=2**24),
-    )(queries, prefix_keys, prefix_values, own_keys, own_values, lengths)
+    )(queries, prefix_keys, prefix_values, jnp.concatenate([own_keys, own_values], axis=0), lengths)
 
 
 def solution(mesh):

time: 36 us -> 35.1 us (0.975)
  local copies, waits for them, and re-layouts: 1.67 us -> 0.71 us
  other arithmetic: 0 us -> 0.78 us
  Pallas kernels: 33.5 us -> 32.8 us
    unnamed x1, local copies, waits for them, and re-layouts: 1.67 us -> 0.71 us
    concatenate x0 -> x1, other arithmetic: none -> 0.78 us  [shards(): jnp.concatenate([own_keys, own_values], axis=0)]
    pallas_call x1, Pallas kernels: 33.5 us -> 32.8 us  [shards(): pl.pallas_call(kernel, out_shape=jax.ShapeDtypeStruct((T, H * D), BF16),...]
where the time goes in v3:
time: 35.1 us; the launch traced here: 35 us
  Pallas kernels  32.8 us (93%)
  other arithmetic  0.78 us (2%)
  local copies, waits for them, and re-layouts  0.71 us (2%)
  between operations  0.66 us (2%)
    pallas_call x1, Pallas kernels, shards(): pl.pallas_call(kernel, out_shape=jax.ShapeDtypeStruct((T, H * D), BF16),...  32.8 us
    concatenate x1, other arithmetic, shards(): jnp.concatenate([own_keys, own_values], axis=0)  0.78 us
    unnamed x1, local copies, waits for them, and re-layouts  0.71 us

profile of v3, /device:TPU:192, one launch (start us, length us, event | category | flops | bytes accessed | tf_op | source)
XLA Modules:
  0.0 35.0 jit_solution(15181017665782054655)
XLA Ops:
  0.7 0.8 %pad_maximum_fusion.okv_hbm = bf16[256,128]{1,0:T(8,128)(2,1)S(1)} fusion(bf16[128,128]{1,0:T(8,128)(2,1)} %param.10, bf16[128,128]{1,0:T(8,128)(2,1)} %param.9), kind=kLoop, calls=%fused_computation | loop fusion | flops 131072 | bytes 131072 | tf_op jit(solution)/shard_map/concatenate | solution.py:290
  1.4 32.8 %shard_map.64 = bf16[128,1024]{1,0:T(8,128)(2,1)S(1)} custom-call(bf16[128,1024]{1,0:T(8,128)(2,1)} %q_hbm.1, bf16[1024,128]{1,0:T(8,128)(2,1)} %k_hbm.1, bf16[1024,128]{1,0:T(8,128)(2,1)} %v_hbm.1, bf16[256,128]{1,0:T(8,128)(2,1)S(1)} %pad_maximum_fusion.okv_hbm, s32[1]{0:T(128)S(6)} %copy.8.len_hbm), custom_call_target="tpu_custom_call" | custom-call | flops 8589934592 | bytes 2097152 | tf_op jit(solution)/shard_map/pallas_call | solution.py:262
  34.3 0.7 %copy.9 = bf16[128,1024]{1,0:T(8,128)(2,1)} copy(bf16[128,1024]{1,0:T(8,128)(2,1)S(1)} %shard_map.64) | data formatting | bytes 524288

commit v4 on v3

--- a/solution.py
+++ b/solution.py
@@ -19,8 +19,7 @@
 SCALE = math.log2(math.e) / math.sqrt(D)
 
 
-ORDER = ((0, 0), (1, 0), (2, 0), (1, 1), (2, 1), (3, 0), (3, 1), (3, 2),
-         (1, 2), (3, 3), (1, 3), (2, 2), (2, 3), (0, 1), (0, 2), (0, 3))
+ORDER = ((0, 0), (1, 0), (2, 0), (1, 1), (2, 1), (3, 0), (3, 1), (3, 2), (3, 3), (1, 2), (1, 3), (2, 2), (2, 3), (0, 1), (0, 2), (0, 3))
 BLOCKS = len(ORDER)
 
 

time: 35.1 us -> 34.3 us (0.977)
  the two profiles are of different devices: /device:TPU:192 before, /device:TPU:1 now
where the time goes in v4:
time: 34.3 us; the launch traced here: 34 us
  Pallas kernels  31.8 us (93%)
  other arithmetic  0.78 us (2%)
  local copies, waits for them, and re-layouts  0.71 us (2%)
  between operations  0.66 us (2%)
    pallas_call x1, Pallas kernels, shards(): pl.pallas_call(kernel, out_shape=jax.ShapeDtypeStruct((T, H * D), BF16),...  31.8 us
    concatenate x1, other arithmetic, shards(): jnp.concatenate([own_keys, own_values], axis=0)  0.78 us
    unnamed x1, local copies, waits for them, and re-layouts  0.71 us

profile of v4, /device:TPU:1, one launch (start us, length us, event | category | flops | bytes accessed | tf_op | source)
XLA Modules:
  0.0 34.0 jit_solution(9106053123874096979)
XLA Ops:
  0.7 0.8 %pad_maximum_fusion.okv_hbm = bf16[256,128]{1,0:T(8,128)(2,1)S(1)} fusion(bf16[128,128]{1,0:T(8,128)(2,1)} %param.10, bf16[128,128]{1,0:T(8,128)(2,1)} %param.9), kind=kLoop, calls=%fused_computation | loop fusion | flops 131072 | bytes 131072 | tf_op jit(solution)/shard_map/concatenate | solution.py:289
  1.4 31.8 %shard_map.64 = bf16[128,1024]{1,0:T(8,128)(2,1)S(1)} custom-call(bf16[128,1024]{1,0:T(8,128)(2,1)} %q_hbm.1, bf16[1024,128]{1,0:T(8,128)(2,1)} %k_hbm.1, bf16[1024,128]{1,0:T(8,128)(2,1)} %v_hbm.1, bf16[256,128]{1,0:T(8,128)(2,1)S(1)} %pad_maximum_fusion.okv_hbm, s32[1]{0:T(128)S(6)} %copy.8.len_hbm), custom_call_target="tpu_custom_call" | custom-call | flops 8589934592 | bytes 2097152 | tf_op jit(solution)/shard_map/pallas_call | solution.py:261
  33.3 0.7 %copy.9 = bf16[128,1024]{1,0:T(8,128)(2,1)} copy(bf16[128,1024]{1,0:T(8,128)(2,1)S(1)} %shard_map.64) | data formatting | bytes 524288

commit v5 on v4

--- a/solution.py
+++ b/solution.py
@@ -171,9 +171,6 @@
         sm[n, 0:1] = jnp.sum(p, axis=0, keepdims=True)
     for u in range(4):
         scores(0, u, s0, x0)
-    for n in range(4):
-        k_copy(n).start()
-        v_copy(n).start()
     loads[6].wait()
 
     even, odd = (s0, x0), (s1, x1)
@@ -218,22 +215,29 @@
         return todo
 
     def body(j, carry):
-        for parity, (cur, nxt) in enumerate(((even, odd), (odd, even))):
+        for parity, (cur, nxt) in enumerate(((odd, even), (even, odd))):
             for k in range(BLOCKS // 2 - 1):
-                todo = before(2 * k + parity)
+                todo = before(1 + 2 * k + parity)
                 if todo:
                     @pl.when(j == k)
                     def _():
                         for act, what in todo:
                             act(what)
-            block(2 * j + parity, cur, nxt)
+            block(1 + 2 * j + parity, cur, nxt)
         return carry
 
+    block(0, even, None)
+    for n in range(4):
+        k_copy(n).start()
+        v_copy(n).start()
+    for act, what in before(0):
+        act(what)
+    for u in range(4):
+        scores(1, u, *odd)
     lax.fori_loop(0, BLOCKS // 2 - 1, body, 0)
-    for i, cur, nxt in ((BLOCKS - 2, even, odd), (BLOCKS - 1, odd, None)):
-        for act, what in before(i):
-            act(what)
-        block(i, cur, nxt)
+    for act, what in before(BLOCKS - 1):
+        act(what)
+    block(BLOCKS - 1, odd, None)
     for unit, n in ((0, 0), (1, 1), (0, 4), (1, 2)):
         merge(unit, n)
 

time: 34.3 us -> 33.9 us (0.988)
  no operation moved by 1% of the time
where the time goes in v5:
time: 33.9 us; the launch traced here: 33.7 us
  Pallas kernels  31.6 us (93%)
  other arithmetic  0.78 us (2%)
  local copies, waits for them, and re-layouts  0.71 us (2%)
  between operations  0.66 us (2%)
    pallas_call x1, Pallas kernels, shards(): pl.pallas_call(kernel, out_shape=jax.ShapeDtypeStruct((T, H * D), BF16),...  31.6 us
    concatenate x1, other arithmetic, shards(): jnp.concatenate([own_keys, own_values], axis=0)  0.78 us
    unnamed x1, local copies, waits for them, and re-layouts  0.71 us

profile of v5, /device:TPU:1, one launch (start us, length us, event | category | flops | bytes accessed | tf_op | source)
XLA Modules:
  0.0 33.7 jit_solution(4333398549181712327)
XLA Ops:
  0.7 0.8 %pad_maximum_fusion.okv_hbm = bf16[256,128]{1,0:T(8,128)(2,1)S(1)} fusion(bf16[128,128]{1,0:T(8,128)(2,1)} %param.10, bf16[128,128]{1,0:T(8,128)(2,1)} %param.9), kind=kLoop, calls=%fused_computation | loop fusion | flops 131072 | bytes 131072 | tf_op jit(solution)/shard_map/concatenate | solution.py:293
  1.4 31.6 %shard_map.64 = bf16[128,1024]{1,0:T(8,128)(2,1)S(1)} custom-call(bf16[128,1024]{1,0:T(8,128)(2,1)} %q_hbm.1, bf16[1024,128]{1,0:T(8,128)(2,1)} %k_hbm.1, bf16[1024,128]{1,0:T(8,128)(2,1)} %v_hbm.1, bf16[256,128]{1,0:T(8,128)(2,1)S(1)} %pad_maximum_fusion.okv_hbm, s32[1]{0:T(128)S(6)} %copy.8.len_hbm), custom_call_target="tpu_custom_call" | custom-call | flops 8589934592 | bytes 2097152 | tf_op jit(solution)/shard_map/pallas_call | solution.py:265
  33.0 0.7 %copy.9 = bf16[128,1024]{1,0:T(8,128)(2,1)} copy(bf16[128,1024]{1,0:T(8,128)(2,1)S(1)} %shard_map.64) | data formatting | bytes 524288

commit v6 on v5

--- a/solution.py
+++ b/solution.py
@@ -76,19 +76,19 @@
 
     def q_copy(n):
         dst, to = 2 + n, (right, left)[n % 2]
-        src = q.at[n - 2] if n > 3 else q_hbm.at[:, half((0, 1, 1, 0)[n])]
+        src = q.at[n - 2 if n > 3 else (0, 1, 1, 0)[n]]
         return remote(src, q.at[dst], q_ssem.at[n], q_rsem.at[n], to)
 
-    def ring_copy(n, hbm, buf, ssem, rsem):
+    def ring_copy(n, buf, ssem, rsem):
         place, to = half(n % 2), (up, down)[n % 2]
-        src = buf.at[1, place] if n > 3 else hbm.at[half((0, 1, 1, 0)[n])]
+        src = buf.at[1, place] if n > 3 else buf.at[0, half((0, 1, 1, 0)[n])]
         return remote(src, buf.at[1 + n // 2, place], ssem.at[n], rsem.at[n], to)
 
     def k_copy(n):
-        return ring_copy(n, k_hbm, kb, k_ssem, k_rsem)
+        return ring_copy(n, kb, k_ssem, k_rsem)
 
     def v_copy(n):
-        return ring_copy(n, v_hbm, vb, v_ssem, v_rsem)
+        return ring_copy(n, vb, v_ssem, v_rsem)
 
     def o_copy(n):
         to = (far, far, right, right, left, left)[n]
@@ -148,6 +148,8 @@
                 scores(i + 1, u, *nxt)
             absorb(i, u, *cur)
 
+    loads[0].wait()
+    loads[1].wait()
     pl.semaphore_wait(barrier, 5)
     for n in range(4):
         q_copy(n).start()
@@ -155,7 +157,7 @@
         acc[n] = jnp.zeros((D, HALF), F32)
         mx[n, 0:1] = jnp.full((1, HALF), -1e30, F32)
         sm[n, 0:1] = jnp.zeros((1, HALF), F32)
-    for n in range(6):
+    for n in range(2, 6):
         loads[n].wait()
 
     length = len_ref[0]

time: 33.9 us -> 33.7 us (level)
  no operation moved by 1% of the time
where the time goes in v6:
time: 33.7 us; the launch traced here: 33.5 us
  Pallas kernels  31.4 us (93%)
  other arithmetic  0.78 us (2%)
  local copies, waits for them, and re-layouts  0.71 us (2%)
  between operations  0.66 us (2%)
    pallas_call x1, Pallas kernels, shards(): pl.pallas_call(kernel, out_shape=jax.ShapeDtypeStruct((T, H * D), BF16),...  31.4 us
    concatenate x1, other arithmetic, shards(): jnp.concatenate([own_keys, own_values], axis=0)  0.78 us
    unnamed x1, local copies, waits for them, and re-layouts  0.71 us

profile of v6, /device:TPU:1, one launch (start us, length us, event | category | flops | bytes accessed | tf_op | source)
XLA Modules:
  0.0 33.5 jit_solution(9791581631169800081)
XLA Ops:
  0.7 0.8 %pad_maximum_fusion.okv_hbm = bf16[256,128]{1,0:T(8,128)(2,1)S(1)} fusion(bf16[128,128]{1,0:T(8,128)(2,1)} %param.10, bf16[128,128]{1,0:T(8,128)(2,1)} %param.9), kind=kLoop, calls=%fused_computation | loop fusion | flops 131072 | bytes 131072 | tf_op jit(solution)/shard_map/concatenate | solution.py:295
  1.4 31.4 %shard_map.64 = bf16[128,1024]{1,0:T(8,128)(2,1)S(1)} custom-call(bf16[128,1024]{1,0:T(8,128)(2,1)} %q_hbm.1, bf16[1024,128]{1,0:T(8,128)(2,1)} %k_hbm.1, bf16[1024,128]{1,0:T(8,128)(2,1)} %v_hbm.1, bf16[256,128]{1,0:T(8,128)(2,1)S(1)} %pad_maximum_fusion.okv_hbm, s32[1]{0:T(128)S(6)} %copy.8.len_hbm), custom_call_target="tpu_custom_call" | custom-call | flops 8589934592 | bytes 2097152 | tf_op jit(solution)/shard_map/pallas_call | solution.py:267
  32.8 0.7 %copy.9 = bf16[128,1024]{1,0:T(8,128)(2,1)} copy(bf16[128,1024]{1,0:T(8,128)(2,1)S(1)} %shard_map.64) | data formatting | bytes 524288

commit v7 on v5

--- a/solution.py
+++ b/solution.py
@@ -245,7 +245,7 @@
     writes = []
     for unit, n in ((0, 3), (1, 5)):
         merge(unit, n)
-        result = acc[unit] / sm[unit, 0:1]
+        result = acc[unit] * (1.0 / sm[unit, 0:1])
         for h in range(4):
             piece = result[:, h * T:(h + 1) * T].T
             out[:, (unit * 4 + h) * D:(unit * 4 + h + 1) * D] = jnp.where(rows < length, piece, 0.0).astype(BF16)

time: 33.9 us -> 33.9 us (level)
  no operation moved by 1% of the time
where the time goes in v7:
time: 33.9 us; the launch traced here: 33.7 us
  Pallas kernels  31.6 us (93%)
  other arithmetic  0.78 us (2%)
  local copies, waits for them, and re-layouts  0.71 us (2%)
  between operations  0.66 us (2%)
    pallas_call x1, Pallas kernels, shards(): pl.pallas_call(kernel, out_shape=jax.ShapeDtypeStruct((T, H * D), BF16),...  31.6 us
    concatenate x1, other arithmetic, shards(): jnp.concatenate([own_keys, own_values], axis=0)  0.78 us
    unnamed x1, local copies, waits for them, and re-layouts  0.71 us

profile of v7, /device:TPU:1, one launch (start us, length us, event | category | flops | bytes accessed | tf_op | source)
XLA Modules:
  0.0 33.7 jit_solution(7564740380254974026)
XLA Ops:
  0.7 0.8 %pad_maximum_fusion.okv_hbm = bf16[256,128]{1,0:T(8,128)(2,1)S(1)} fusion(bf16[128,128]{1,0:T(8,128)(2,1)} %param.10, bf16[128,128]{1,0:T(8,128)(2,1)} %param.9), kind=kLoop, calls=%fused_computation | loop fusion | flops 131072 | bytes 131072 | tf_op jit(solution)/shard_map/concatenate | solution.py:293
  1.4 31.6 %shard_map.64 = bf16[128,1024]{1,0:T(8,128)(2,1)S(1)} custom-call(bf16[128,1024]{1,0:T(8,128)(2,1)} %q_hbm.1, bf16[1024,128]{1,0:T(8,128)(2,1)} %k_hbm.1, bf16[1024,128]{1,0:T(8,128)(2,1)} %v_hbm.1, bf16[256,128]{1,0:T(8,128)(2,1)S(1)} %pad_maximum_fusion.okv_hbm, s32[1]{0:T(128)S(6)} %copy.8.len_hbm), custom_call_target="tpu_custom_call" | custom-call | flops 8589934592 | bytes 2097152 | tf_op jit(solution)/shard_map/pallas_call | solution.py:265
  33.0 0.7 %copy.9 = bf16[128,1024]{1,0:T(8,128)(2,1)} copy(bf16[128,1024]{1,0:T(8,128)(2,1)S(1)} %shard_map.64) | data formatting | bytes 524288
